TPU v7x, 256 devices: a whole 4x4x8 slice. The times are simulated.
256 devices in a mesh: dp: 32 (over y_hi, z, core), mp: 8 (over y_lo, x).
Axes of the slice: x: 4, y: 4 (y_hi: 2, y_lo: 2; y = y_hi * 2 + y_lo), z: 8, core: 2. Of those that a mesh axis runs over, the one named last changes fastest.
Arguments:
- d_out: bfloat16 [4096, 8192], P(('dp', 'mp')), may hold values from -24 to 24
- gate_pre: bfloat16 [4096, 14336], P('dp', 'mp'), may hold values from -6 to 6
- up_pre: bfloat16 [4096, 14336], P('dp', 'mp'), may hold values from -6 to 6
- down_weight: bfloat16 [14336, 8192], P('mp', 'dp'), may hold values from -0.046875 to 0.046875
Outputs:
- grad_gate: bfloat16 [4096, 14336], P('dp', 'mp')
- grad_up: bfloat16 [4096, 14336], P('dp', 'mp')
- grad_down: float32 [14336, 8192], P('mp', 'dp')
All inputs are finite; a program needn't handle non-finite values.
Results may differ from a plain program's by a relative error of at most 0.035.
Values may be sent and summed in bfloat16 or wider, within the bound.
A program may use at most 64 MiB of HBM per device.

v0:
```python
import jax
import jax.numpy as jnp
from jax import lax
from jax.sharding import PartitionSpec as P


def gated_product(gate_piece, up_piece):
    gate_vals = gate_piece.astype(jnp.float32)
    return (gate_vals * jax.nn.sigmoid(gate_vals) * up_piece.astype(jnp.float32)).astype(
        jnp.bfloat16
    )


def on_device(d_out, gate_pre, up_pre, down_weight):
    group_grad = lax.all_gather(d_out, "mp", axis=0, tiled=True)
    columns = lax.all_to_all(group_grad, "dp", split_axis=1, concat_axis=0, tiled=True)
    d_hidden = lax.psum_scatter(
        lax.dot_general(
            columns, down_weight, (((1,), (1,)), ((), ())), preferred_element_type=jnp.float32
        ).astype(jnp.bfloat16),
        "dp",
        scatter_dimension=0,
        tiled=True,
    ).astype(jnp.float32)
    hidden = gated_product(gate_pre, up_pre)
    grad_down = lax.dot_general(
        lax.all_gather(hidden, "dp", axis=0, tiled=True),
        columns,
        (((0,), (0,)), ((), ())),
        preferred_element_type=jnp.float32,
    )
    gate_vals = gate_pre.astype(jnp.float32)
    up_vals = up_pre.astype(jnp.float32)
    sgate = jax.nn.sigmoid(gate_vals)
    grad_up = (d_hidden * gate_vals * sgate).astype(jnp.bfloat16)
    grad_gate = (d_hidden * up_vals * sgate * (1.0 + gate_vals * (1.0 - sgate))).astype(
        jnp.bfloat16
    )
    return (grad_gate, grad_up, grad_down)


def solution(mesh):
    placed = (P(("dp", "mp"), None), P("dp", "mp"), P("dp", "mp"), P("mp", "dp"))
    return jax.shard_map(
        on_device,
        mesh=mesh,
        in_specs=placed,
        out_specs=(P("dp", "mp"), P("dp", "mp"), P("mp", "dp")),
        check_vma=False,
    )
```

profile of v0, /device:TPU:1, one launch (start us, length us, event | category | flops | bytes accessed | tf_op | source)
XLA Modules:
  0.0 456.6 jit_solution(5653199185678427213)
XLA Ops:
  7.2 0.0 copy-start
  7.2 0.0 all-gather.3.cloned.1.call-start
  7.2 0.7 all-gather.3.cloned.1.call-update
  7.9 0.0 reduce-scatter.2.cloned.1.call-start
  8.0 44.5 %all-gather.3.cloned.1.call-done = bf16[128,8192]{1,0:T(8,128)(2,1)} async-done(((bf16[16,8192]{1,0:T(8,128)(2,1)}), bf16[128,8192]{1,0:T(8,128)(2,1)}) %all-gather.3.cloned.1.call-update) | async-done | bytes 2097168 | tf_op jit(solution)/shard_map/all_gather | solution.py:15
  52.4 3.2 copy.9
  55.7 65.2 %all_to_all.19 = bf16[128,32,256]{0,2,1:T(8,128)(2,1)} all-to-all(bf16[128,32,256]{0,2,1:T(8,128)(2,1)S(1)} %bitcast.9), channel_id=1, replica_groups=mesh['dp'=32,'mp'=8] {'dp'}, dimensions={1} | all-to-all | bytes 4194304 | tf_op jit(solution)/shard_map/all_to_all | solution.py:16
  120.8 3.3 copy.10
  124.1 0.0 copy-done
  124.1 7.3 %convolution_convert_fusion = bf16[4096,1792]{1,0:T(8,128)(2,1)} fusion(bf16[4096,256]{1,0:T(8,128)(2,1)S(1)} %bitcast.7, bf16[1792,256]{1,0:T(8,128)(2,1)S(1)} %copy-done), kind=kOutput, calls=%fused_computation | convolution fusion | flops 3765436416 | bytes 17694720 | tf_op jit(solution)/shard_map/dot_general | solution.py:18
  131.5 0.0 copy-start.1
  131.5 0.0 reduce-scatter.2.cloned.1.call-update
  131.5 0.0 all-gather.5.cloned.1.call-start
  131.5 176.4 %reduce-scatter.2.cloned.1.call-done = bf16[128,1792]{1,0:T(8,128)(2,1)} async-done(((bf16[4096,1792]{1,0:T(8,128)(2,1)}), bf16[128,1792]{1,0:T(8,128)(2,1)}) %reduce-scatter.2.cloned.1.call-update) | async-done | bytes 458768 | tf_op jit(solution)/shard_map/reduce_scatter | solution.py:17
  307.9 0.0 copy-done.1
  307.9 2.7 fusion.3
  310.6 0.0 all-gather.5.cloned.1.call-update
  310.7 130.9 %all-gather.5.cloned.1.call-done = bf16[4096,1792]{1,0:T(8,128)(2,1)} async-done(((bf16[128,1792]{1,0:T(8,128)(2,1)}), bf16[4096,1792]{1,0:T(8,128)(2,1)}) %all-gather.5.cloned.1.call-update) | async-done | bytes 14680080 | tf_op jit(solution)/shard_map/all_gather | solution.py:27
  441.5 8.6 %fusion.10 = f32[1792,256]{1,0:T(8,128)} fusion(bf16[4096,1792]{1,0:T(8,128)(2,1)} %all-gather.5.cloned.1.call-done, bf16[4096,256]{1,0:T(8,128)(2,1)S(1)} %bitcast.8), kind=kOutput, calls=%fused_computation.17 | convolution fusion | flops 3758096384 | bytes 18612224 | tf_op jit(solution)/shard_map/dot_general | solution.py:26
Async XLA Ops:
  7.2 116.9 %copy-start = (bf16[1792,256]{1,0:T(8,128)(2,1)S(1)}, bf16[1792,256]{1,0:T(8,128)(2,1)}, u32[]{:S(2)}) copy-start(bf16[1792,256]{1,0:T(8,128)(2,1)} %param.7) | copy-start | bytes 2752516
  7.2 45.3 %all-gather.3.cloned.1.call-start = ((), (), s32[]{:S(2)}) async-start(), calls=%async_computation.2 | async-start | bytes 2359296 | tf_op jit(solution)/shard_map/all_gather | solution.py:15
  7.9 300.0 %reduce-scatter.2.cloned.1.call-start = ((), (), s32[]{:S(2)}) async-start(), calls=%async_computation.3 | async-start | bytes 15138816 | tf_op jit(solution)/shard_map/reduce_scatter | solution.py:17
  131.5 176.5 %copy-start.1 = (bf16[128,1792]{1,0:T(8,128)(2,1)S(1)}, bf16[128,1792]{1,0:T(8,128)(2,1)}, u32[]{:S(2)}) copy-start(bf16[128,1792]{1,0:T(8,128)(2,1)} %param.6) | copy-start | bytes 1376260
  131.5 310.1 %all-gather.5.cloned.1.call-start = ((), (), s32[]{:S(2)}) async-start(), calls=%async_computation.4 | async-start | bytes 15138816 | tf_op jit(solution)/shard_map/all_gather | solution.py:27
Sparse Core Ops, SparseCore 0:
  9.8 42.5 all-gather.2
  131.6 176.2 reduce-scatter.1
  311.7 129.8 all-gather.4
where the time goes:
time: 457 us
  waiting for transfers between devices  352 us (77%)
  blocking collectives  65.2 us (14%)
  matrix products  15.9 us (3%)
  between operations  13.8 us (3%)
  local copies, waits for them, and re-layouts  6.49 us (1%)
    reduce_scatter x1, waiting for transfers between devices, on_device(): lax.psum_scatter(lax.dot_general(columns, down_weight, (((1,), (1,)), (()...  176 us
    all_gather x1, waiting for transfers between devices, on_device(): lax.all_gather(hidden, 'dp', axis=0, tiled=True)  131 us
    all_to_all x1, blocking collectives, on_device(): lax.all_to_all(group_grad, 'dp', split_axis=1, concat_axis=0, tiled=True)  65.2 us
    all_gather x1, waiting for transfers between devices, on_device(): group_grad = lax.all_gather(d_out, 'mp', axis=0, tiled=True)  44.5 us
  transfers between devices with their start and end apart: 3, of which 3 were waited for; matrix products, arithmetic and copies ran while one was open for 0% of the time, Pallas kernels for 0%

commit v1 on v0

v1 whole, which is shorter than its diff:
```python
import jax
import jax.numpy as jnp
from jax import lax
from jax.experimental import pallas as pl
from jax.experimental.pallas import tpu as pltpu
from jax.sharding import PartitionSpec as P

MESH = pl.DeviceIdType.MESH
TOK, F, DB, HF = 128, 1792, 256, 896
D = 8192


def kernel(
    d_ref, g_ref, u_ref, w_ref, gg_ref, gu_ref, gd_ref,
    gv, uv, s1, s2, xb, ht, wb, dh, rra, rrb, rla, rlb, cs, cr, k0, k1, ys, yr,
    lsem, xs, xr, ags, agr, rss, rsr, ws, wr, gs, gr,
):
    g, m = lax.axis_index("dp"), lax.axis_index("mp")
    yh, z, c = g // 16, (g // 2) % 8, g % 2
    yl, x = m // 4, m % 4

    def zdev(k):
        return ((yh * 8 + (z + k) % 8) * 2 + c, m)

    def xdev(k):
        return (g, yl * 4 + (x + k) % 4)

    ydev = (((1 - yh) * 8 + z) * 2 + c, m)
    cdev = ((yh * 8 + z) * 2 + 1 - c, m)
    ldev = (g, (1 - yl) * 4 + x)

    sent = []

    def send(src, dst, ssem, rsem, to):
        cp = pltpu.make_async_remote_copy(
            src_ref=src, dst_ref=dst, send_sem=ssem, recv_sem=rsem, device_id=to, device_id_type=MESH
        )
        cp.start()
        sent.append(cp)
        return cp

    barrier = pltpu.get_barrier_semaphore()
    friends = [zdev(k) for k in range(1, 8)] + [xdev(1), xdev(3), ydev, cdev, ldev]
    for f in friends:
        pl.semaphore_signal(barrier, inc=1, device_id=f, device_id_type=MESH)

    cpg = pltpu.make_async_copy(g_ref, gv, lsem.at[0])
    cpu = pltpu.make_async_copy(u_ref, uv, lsem.at[1])
    own_b = pl.ds(pl.multiple_of((yh * 2 + c) * DB, DB), DB)
    oth_b = pl.ds(pl.multiple_of(((1 - yh) * 2 + c) * DB, DB), DB)
    cpw = pltpu.make_async_copy(w_ref, wb.at[:, own_b], lsem.at[2])
    cpg.start()
    cpu.start()
    cpw.start()
    myrows = pl.ds(pl.multiple_of(m * 16, 16), 16)
    cpx = []
    for h in range(2):
        cols = pl.ds(pl.multiple_of(h * 4096 + z * 512, 512), 512)
        cp = pltpu.make_async_copy(
            d_ref.at[:, cols], xb.at[z, myrows, pl.ds(h * 512, 512)], lsem.at[3 + h]
        )
        cp.start()
        cpx.append(cp)

    def ht_cols(k):
        return pl.ds(pl.multiple_of(((z + k) % 8) * TOK, TOK), TOK)

    cpg.wait()
    cpu.wait()

    @pl.loop(0, F // 256)
    def _(i):
        sl = pl.ds(pl.multiple_of(i * 256, 256), 256)
        gate = gv[:, sl].astype(jnp.float32)
        up = uv[:, sl].astype(jnp.float32)
        sig = jax.nn.sigmoid(gate)
        a = gate * sig
        s1[:, sl] = a
        s2[:, sl] = up * sig * (1.0 + gate * (1.0 - sig))
        ht[sl, ht_cols(0)] = (a * up).T.astype(jnp.bfloat16)

    pl.semaphore_wait(barrier, len(friends))

    a2a = []
    for k in (4, 3, 5, 2, 6, 1, 7):
        for h in range(2):
            cols = pl.ds(pl.multiple_of(h * 4096 + ((z + k) % 8) * 512, 512), 512)
            i = (k - 1) * 2 + h
            a2a.append(
                send(
                    d_ref.at[:, cols], xb.at[z, myrows, pl.ds(h * 512, 512)],
                    xs.at[i], xr.at[i], zdev(k),
                )
            )

    wy = send(w_ref, wb.at[:, own_b], ws.at[0], wr.at[0], ydev)
    wc = [send(w_ref, wb.at[:, own_b], ws.at[1], wr.at[1], cdev)]

    half = [pl.ds(0, HF), pl.ds(HF, HF)]
    agright, agleft = [], []

    def ag(lst, k, hh, to, base):
        i = base + len(lst)
        lst.append(
            send(ht.at[half[hh], ht_cols(k)], ht.at[half[hh], ht_cols(k)], ags.at[i], agr.at[i], to)
        )

    for hh in range(2):
        ag(agright, 0, hh, zdev(1), 0)
        ag(agleft, 0, 1 - hh, zdev(7), 7)

    def ag_event(k):
        agright[k].wait_recv()
        agleft[k].wait_recv()
        if k < 5:
            ag(agright, -(k // 2 + 1), k % 2, zdev(1), 0)
            ag(agleft, k // 2 + 1, 1 - k % 2, zdev(7), 7)

    for cp in cpx:
        cp.wait()
    for cp in a2a:
        cp.wait_recv()

    def slot(l, xx):
        return xb.at[:, pl.ds(pl.multiple_of((l * 4 + xx % 4) * 16, 16), 16), :]

    def xsend(l, xx, i, to):
        return send(slot(l, xx), slot(l, xx), xs.at[14 + i], xr.at[14 + i], to)

    xy = xsend(yl, x, 0, ldev)
    xa = [xsend(yl, x, 1, xdev(1)), xsend(yl, x, 2, xdev(3))]
    ag_event(0)
    xy.wait_recv()
    xa += [xsend(1 - yl, x, 3, xdev(1)), xsend(1 - yl, x, 4, xdev(3))]
    ag_event(1)
    for cp in xa:
        cp.wait_recv()
    xf = [xsend(0, x + 3, 5, xdev(1)), xsend(1, x + 1, 6, xdev(3))]
    ag_event(2)
    wy.wait_recv()
    wc.append(send(wb.at[:, oth_b], wb.at[:, oth_b], ws.at[2], wr.at[2], cdev))
    ag_event(3)
    for cp in xf:
        cp.wait_recv()
    cpw.wait()
    for cp in wc:
        cp.wait_recv()
    ag_event(4)

    @pl.loop(0, F // 256)
    def _(i):
        sl = pl.ds(pl.multiple_of(i * 256, 256), 256)
        r = lax.dot_general(
            xb[...].reshape(8 * TOK, 1024), wb[sl, :], (((1,), (1,)), ((), ())),
            preferred_element_type=jnp.float32,
        )
        dh[:, :, sl] = r.astype(jnp.bfloat16).reshape(8, TOK, 256)

    rsright, rsleft = [], []
    rbuf = {("r", 0): rra, ("r", 1): rrb, ("l", 0): rla, ("l", 1): rlb}

    def rs(right):
        lst = rsright if right else rsleft
        i = len(lst)
        hh = i % 2 if right else 1 - i % 2
        k = 4 - (i + 1) // 2
        buf = rbuf[("r" if right else "l", hh)]
        j = i + (0 if right else 7)
        lst.append(
            send(
                dh.at[(z + (k if right else -k)) % 8, :, half[hh]], buf.at[i // 2],
                rss.at[j], rsr.at[j], zdev(1) if right else zdev(7),
            )
        )

    for _ in range(2):
        rs(True)
        rs(False)

    def rs_event(i):
        for right in (True, False):
            (rsright if right else rsleft)[i].wait_recv()
            if i < 5:
                hh = i % 2 if right else 1 - i % 2
                k = 3 - (i + 1) // 2
                at = (z + (k if right else -k)) % 8
                buf = rbuf[("r" if right else "l", hh)]
                dh[at, :, half[hh]] = (
                    dh[at, :, half[hh]].astype(jnp.float32)
                    + buf[i // 2].astype(jnp.float32)
                ).astype(jnp.bfloat16)
                rs(right)

    ag_event(5)
    ag_event(6)

    def block(by, bc, h):
        cols = pl.ds(pl.multiple_of((by * 2 + bc) * DB, DB), DB)
        return jnp.dot(
            ht[pl.ds(pl.multiple_of(h * HF, HF), HF), :],
            xb[:, :, cols].reshape(8 * TOK, DB),
            preferred_element_type=jnp.float32,
        )

    def hrows(h):
        return pl.ds(pl.multiple_of(h * HF, HF), HF)

    def to_core(n, by):
        cps = []

        @pl.loop(0, 2)
        def _(h):
            cs[n, hrows(h), :] = block(by, 1 - c, h).astype(jnp.bfloat16)

        for h in range(2):
            cps.append(
                send(cs.at[n, half[h], :], cr.at[n, half[h], :], gs.at[2 * n + h], gr.at[2 * n + h], cdev)
            )
        return cps

    def keep(k, by):
        @pl.loop(0, 2)
        def _(h):
            k[hrows(h), :] = block(by, c, h)

    c0 = to_core(0, 1 - yh)
    keep(k0, 1 - yh)
    yy = []
    for h in range(2):
        c0[h].wait_recv()
        ys[half[h], :] = (k0[half[h], :] + cr[0, half[h], :].astype(jnp.float32)).astype(jnp.bfloat16)
        yy.append(send(ys.at[half[h], :], yr.at[half[h], :], gs.at[4 + h], gr.at[4 + h], ydev))
    rs_event(0)
    c1 = to_core(1, yh)
    keep(k1, yh)
    rs_event(1)
    for h in range(2):
        c1[h].wait_recv()
        k1[half[h], :] += cr[1, half[h], :].astype(jnp.float32)
    rs_event(2)
    rs_event(3)
    rs_event(4)
    yy[0].wait_recv()
    gd_ref[half[0], :] = k1[half[0], :] + yr[half[0], :].astype(jnp.float32)
    yy[1].wait_recv()
    gd_ref[half[1], :] = k1[half[1], :] + yr[half[1], :].astype(jnp.float32)
    rs_event(5)
    rs_event(6)
    for hh in range(2):
        total = (
            dh[z, :, half[hh]].astype(jnp.float32)
            + rbuf[("r", hh)][3 - hh].astype(jnp.float32)
            + rbuf[("l", hh)][2 + hh].astype(jnp.float32)
        )
        gu_ref[:, half[hh]] = (total * s1[:, half[hh]]).astype(jnp.bfloat16)
        gg_ref[:, half[hh]] = (total * s2[:, half[hh]]).astype(jnp.bfloat16)
    for cp in sent:
        cp.wait_send()


def on_device(d_out, gate_pre, up_pre, down_weight):
    bf, f32 = jnp.bfloat16, jnp.float32
    hbm = pl.BlockSpec(memory_space=pl.ANY)
    vm = pl.BlockSpec(memory_space=pltpu.VMEM)
    V = pltpu.VMEM
    dma = pltpu.SemaphoreType.DMA
    return pl.pallas_call(
        kernel,
        out_shape=(
            jax.ShapeDtypeStruct((TOK, F), bf),
            jax.ShapeDtypeStruct((TOK, F), bf),
            jax.ShapeDtypeStruct((F, DB), f32),
        ),
        in_specs=[hbm] * 4,
        out_specs=(vm, vm, vm),
        scratch_shapes=[
            V((TOK, F), bf), V((TOK, F), bf), V((TOK, F), f32), V((TOK, F), f32),
            V((8, TOK, 1024), bf), V((F, 1024), bf), V((F, 1024), bf), V((8, TOK, F), bf),
            V((4, TOK, HF), bf), V((3, TOK, HF), bf), V((3, TOK, HF), bf), V((4, TOK, HF), bf),
            V((2, F, DB), bf), V((2, F, DB), bf), V((F, DB), f32), V((F, DB), f32),
            V((F, DB), bf), V((F, DB), bf),
            dma((5,)), dma((21,)), dma((21,)), dma((14,)), dma((14,)), dma((14,)), dma((14,)),
            dma((3,)), dma((3,)), dma((6,)), dma((6,)),
        ],
        compiler_params=pltpu.CompilerParams(
            collective_id=0, has_side_effects=True, vmem_limit_bytes=60 << 20
        ),
        cost_estimate=pl.CostEstimate(
            flops=4 * 1024 * 1024 * F, bytes_accessed=6 << 20, transcendentals=TOK * F
        ),
        name="glu_down_backward",
    )(d_out, gate_pre, up_pre, down_weight)


def solution(mesh):
    return jax.shard_map(
        on_device,
        mesh=mesh,
        in_specs=(P(("dp", "mp"), None), P("dp", "mp"), P("dp", "mp"), P("mp", "dp")),
        out_specs=(P("dp", "mp"), P("dp", "mp"), P("mp", "dp")),
        check_vma=False,
    )
```

time: 457 us -> 102 us (0.22)
  waiting for transfers between devices: 352 us -> 0 us
  Pallas kernels: 0 us -> 96.1 us
  blocking collectives: 65.2 us -> 0 us
  matrix products: 15.9 us -> 0 us
  between operations: 13.8 us -> 0.65 us
    reduce_scatter x1 -> x0, waiting for transfers between devices: 176 us -> none  [on_device(): lax.psum_scatter(lax.dot_general(columns, down_weight, (((1,), (1,)), (()...]
    all_gather x2 -> x0, waiting for transfers between devices: 175 us -> none  [the longest x1 131 us: on_device(): lax.all_gather(hidden, 'dp', axis=0, tiled=True)]
    pallas_call x0 -> x1, Pallas kernels: none -> 96.1 us  [on_device(): pl.pallas_call(kernel, out_shape=(jax.ShapeDtypeStruct((TOK, F), bf), jax...]
    all_to_all x1 -> x0, blocking collectives: 65.2 us -> none  [on_device(): lax.all_to_all(group_grad, 'dp', split_axis=1, concat_axis=0, tiled=True)]
    dot_general x2 -> x0, matrix products: 15.9 us -> none  [the longest x1 8.55 us: on_device(): lax.dot_general(lax.all_gather(hidden, 'dp', axis=0, tiled=True), columns...]
    unnamed x4 -> x5, local copies, waits for them, and re-layouts: 0.01 us -> 5 us
  transfers between devices with their start and end apart: 3 -> 0, of which waited for: 3 -> 0; matrix products, arithmetic and copies ran while one was open for 0% -> 0% of each run, Pallas kernels for 0% -> 0%
where the time goes in v1:
time: 102 us
  Pallas kernels  96.1 us (94%)
  local copies, waits for them, and re-layouts  5 us (5%)
    pallas_call x1, Pallas kernels, on_device(): pl.pallas_call(kernel, out_shape=(jax.ShapeDtypeStruct((TOK, F), bf), jax...  96.1 us
    unnamed x5, local copies, waits for them, and re-layouts  5 us

profile of v1, /device:TPU:1, one launch (start us, length us, event | category | flops | bytes accessed | tf_op | source)
XLA Modules:
  0.0 101.8 jit_solution(16929291021736190386)
XLA Ops:
  0.6 96.1 %glu_down_backward.1 = (bf16[128,1792]{1,0:T(8,128)(2,1)}, bf16[128,1792]{1,0:T(8,128)(2,1)}, f32[1792,256]{1,0:T(8,128)}) custom-call(bf16[16,8192]{1,0:T(8,128)(2,1)} %d_ref.1, bf16[128,1792]{1,0:T(8,128)(2,1)} %g_ref.1, bf16[128,1792]{1,0:T(8,128)(2,1)} %u_ref.1, bf16[1792,256]{1,0:T(8,128)(2,1)} %w_ref.1), custom_call_target="tpu_custom_call" | custom-call | flops 7516192768 | bytes 6291456 | tf_op jit(solution)/shard_map/glu_down_backward/pallas_call | solution.py:267
  96.8 0.0 copy-start
  96.8 1.9 %copy.10 = bf16[128,1792]{1,0:T(8,128)(2,1)} copy(bf16[128,1792]{1,0:T(8,128)(2,1)} %get-tuple-element.6) | data formatting | bytes 917504
  98.7 1.8 %copy.11 = bf16[128,1792]{1,0:T(8,128)(2,1)} copy(bf16[128,1792]{1,0:T(8,128)(2,1)} %get-tuple-element.7) | data formatting | bytes 917504
  100.6 0.0 copy-done
  100.6 1.2 %copy.12 = f32[1792,256]{1,0:T(8,128)} copy(f32[1792,256]{1,0:T(8,128)S(1)} %copy-done) | data formatting | bytes 3670016
Async XLA Ops:
  96.8 3.8 %copy-start = (f32[1792,256]{1,0:T(8,128)S(1)}, f32[1792,256]{1,0:T(8,128)}, u32[]{:S(2)}) copy-start(f32[1792,256]{1,0:T(8,128)} %get-tuple-element.8) | copy-start | bytes 5505028

commit v2 on v1

--- a/solution.py
+++ b/solution.py
@@ -12,7 +12,7 @@
 
 def kernel(
     d_ref, g_ref, u_ref, w_ref, gg_ref, gu_ref, gd_ref,
-    gv, uv, s1, s2, xb, ht, wb, dh, rra, rrb, rla, rlb, cs, cr, k0, k1, ys, yr,
+    gv, uv, s1, s2, xb, ht, wb, dh, rra, rrb, rla, rlb, cs, cr, k0, ys, yr,
     lsem, xs, xr, ags, agr, rss, rsr, ws, wr, gs, gr,
 ):
     g, m = lax.axis_index("dp"), lax.axis_index("mp")
@@ -93,8 +93,12 @@
                 )
             )
 
-    wy = send(w_ref, wb.at[:, own_b], ws.at[0], wr.at[0], ydev)
-    wc = [send(w_ref, wb.at[:, own_b], ws.at[1], wr.at[1], cdev)]
+    def wsend_y(i):
+        rows = (pl.ds(0, 768), pl.ds(768, 1024))[i]
+        return send(w_ref.at[rows], wb.at[rows, own_b], ws.at[i], wr.at[i], ydev)
+
+    wy = [wsend_y(0)]
+    wc = [send(w_ref, wb.at[:, own_b], ws.at[2], wr.at[2], cdev)]
 
     half = [pl.ds(0, HF), pl.ds(HF, HF)]
     agright, agleft = [], []
@@ -131,21 +135,25 @@
     xa = [xsend(yl, x, 1, xdev(1)), xsend(yl, x, 2, xdev(3))]
     ag_event(0)
     xy.wait_recv()
-    xa += [xsend(1 - yl, x, 3, xdev(1)), xsend(1 - yl, x, 4, xdev(3))]
+    xb2 = [xsend(1 - yl, x, 3, xdev(1)), xsend(1 - yl, x, 4, xdev(3))]
+    wy.append(wsend_y(1))
+    for cp in xa:
+        cp.wait_recv()
+    xf = [xsend(yl, x + 3, 5, xdev(1))]
     ag_event(1)
-    for cp in xa:
-        cp.wait_recv()
-    xf = [xsend(0, x + 3, 5, xdev(1)), xsend(1, x + 1, 6, xdev(3))]
+    for cp in xb2:
+        cp.wait_recv()
+    xf.append(xsend(1 - yl, x + 1, 6, xdev(3)))
     ag_event(2)
-    wy.wait_recv()
-    wc.append(send(wb.at[:, oth_b], wb.at[:, oth_b], ws.at[2], wr.at[2], cdev))
+    for cp in wy:
+        cp.wait_recv()
+    wc.append(send(wb.at[:, oth_b], wb.at[:, oth_b], ws.at[3], wr.at[3], cdev))
     ag_event(3)
     for cp in xf:
         cp.wait_recv()
     cpw.wait()
     for cp in wc:
         cp.wait_recv()
-    ag_event(4)
 
     @pl.loop(0, F // 256)
     def _(i):
@@ -156,6 +164,7 @@
         )
         dh[:, :, sl] = r.astype(jnp.bfloat16).reshape(8, TOK, 256)
 
+    ag_event(4)
     rsright, rsleft = [], []
     rbuf = {("r", 0): rra, ("r", 1): rrb, ("l", 0): rla, ("l", 1): rlb}
 
@@ -232,18 +241,21 @@
         yy.append(send(ys.at[half[h], :], yr.at[half[h], :], gs.at[4 + h], gr.at[4 + h], ydev))
     rs_event(0)
     c1 = to_core(1, yh)
-    keep(k1, yh)
+    keep(gd_ref, yh)
     rs_event(1)
     for h in range(2):
         c1[h].wait_recv()
-        k1[half[h], :] += cr[1, half[h], :].astype(jnp.float32)
+        gd_ref[half[h], :] += cr[1, half[h], :].astype(jnp.float32)
     rs_event(2)
     rs_event(3)
     rs_event(4)
     yy[0].wait_recv()
-    gd_ref[half[0], :] = k1[half[0], :] + yr[half[0], :].astype(jnp.float32)
+    def down(h):
+        gd_ref[half[h], :] += yr[half[h], :].astype(jnp.float32)
+
+    down(0)
     yy[1].wait_recv()
-    gd_ref[half[1], :] = k1[half[1], :] + yr[half[1], :].astype(jnp.float32)
+    down(1)
     rs_event(5)
     rs_event(6)
     for hh in range(2):
@@ -258,29 +270,41 @@
         cp.wait_send()
 
 
+def hand_out(a, b, c, ao, bo, co, sem):
+    cps = [pltpu.make_async_copy(a, ao, sem.at[0]), pltpu.make_async_copy(b, bo, sem.at[1])]
+    for i in range(4):
+        rows = pl.ds(i * (F // 4), F // 4)
+        cps.append(pltpu.make_async_copy(c.at[rows], co.at[rows], sem.at[2 + i]))
+    for cp in cps:
+        cp.start()
+    for cp in cps:
+        cp.wait()
+
+
 def on_device(d_out, gate_pre, up_pre, down_weight):
     bf, f32 = jnp.bfloat16, jnp.float32
     hbm = pl.BlockSpec(memory_space=pl.ANY)
-    vm = pl.BlockSpec(memory_space=pltpu.VMEM)
     V = pltpu.VMEM
+    vm = pl.BlockSpec(memory_space=V)
     dma = pltpu.SemaphoreType.DMA
-    return pl.pallas_call(
+    shapes = (
+        jax.ShapeDtypeStruct((TOK, F), bf),
+        jax.ShapeDtypeStruct((TOK, F), bf),
+        jax.ShapeDtypeStruct((F, DB), f32),
+    )
+    res = pl.pallas_call(
         kernel,
-        out_shape=(
-            jax.ShapeDtypeStruct((TOK, F), bf),
-            jax.ShapeDtypeStruct((TOK, F), bf),
-            jax.ShapeDtypeStruct((F, DB), f32),
-        ),
+        out_shape=tuple(V(t.shape, t.dtype) for t in shapes),
         in_specs=[hbm] * 4,
         out_specs=(vm, vm, vm),
         scratch_shapes=[
             V((TOK, F), bf), V((TOK, F), bf), V((TOK, F), f32), V((TOK, F), f32),
             V((8, TOK, 1024), bf), V((F, 1024), bf), V((F, 1024), bf), V((8, TOK, F), bf),
             V((4, TOK, HF), bf), V((3, TOK, HF), bf), V((3, TOK, HF), bf), V((4, TOK, HF), bf),
-            V((2, F, DB), bf), V((2, F, DB), bf), V((F, DB), f32), V((F, DB), f32),
+            V((2, F, DB), bf), V((2, F, DB), bf), V((F, DB), f32),
             V((F, DB), bf), V((F, DB), bf),
             dma((5,)), dma((21,)), dma((21,)), dma((14,)), dma((14,)), dma((14,)), dma((14,)),
-            dma((3,)), dma((3,)), dma((6,)), dma((6,)),
+            dma((4,)), dma((4,)), dma((6,)), dma((6,)),
         ],
         compiler_params=pltpu.CompilerParams(
             collective_id=0, has_side_effects=True, vmem_limit_bytes=60 << 20
@@ -290,6 +314,15 @@
         ),
         name="glu_down_backward",
     )(d_out, gate_pre, up_pre, down_weight)
+    return pl.pallas_call(
+        hand_out,
+        out_shape=shapes,
+        in_specs=[vm] * 3,
+        out_specs=(hbm, hbm, hbm),
+        scratch_shapes=[dma((6,))],
+        compiler_params=pltpu.CompilerParams(vmem_limit_bytes=1 << 20),
+        name="hand_out",
+    )(*res)
 
 
 def solution(mesh):

time: 102 us -> 90.3 us (0.89)
  Pallas kernels: 96.1 us -> 89.5 us
  local copies, waits for them, and re-layouts: 5 us -> 0 us
    pallas_call x1 -> x2, Pallas kernels: 96.1 us -> 89.5 us  [the longest x1 88 us: on_device(): pl.pallas_call(kernel, out_shape=tuple((V(t.shape, t.dtype) for t in shap...]
    unnamed x5 -> x0, local copies, waits for them, and re-layouts: 5 us -> none
where the time goes in v2:
time: 90.3 us; the launch traced here: 90.2 us
  Pallas kernels  89.5 us (99%)
    pallas_call x1, Pallas kernels, on_device(): pl.pallas_call(kernel, out_shape=tuple((V(t.shape, t.dtype) for t in shap...  88 us

profile of v2, /device:TPU:1, one launch (start us, length us, event | category | flops | bytes accessed | tf_op | source)
XLA Modules:
  0.0 90.2 jit_solution(4720275170224349666)
XLA Ops:
  0.6 88.0 %glu_down_backward.1 = (bf16[128,1792]{1,0:T(8,128)(2,1)S(1)}, bf16[128,1792]{1,0:T(8,128)(2,1)S(1)}, f32[1792,256]{1,0:T(8,128)S(1)}) custom-call(bf16[16,8192]{1,0:T(8,128)(2,1)} %d_ref.1, bf16[128,1792]{1,0:T(8,128)(2,1)} %g_ref.1, bf16[128,1792]{1,0:T(8,128)(2,1)} %u_ref.1, bf16[1792,256]{1,0:T(8,128)(2,1)} %w_ref.1), custom_call_target="tpu_custom_call" | custom-call | flops 7516192768 | bytes 6291456 | tf_op jit(solution)/shard_map/glu_down_backward/pallas_call | solution.py:295
  88.6 1.6 %hand_out.1 = (bf16[128,1792]{1,0:T(8,128)(2,1)}, bf16[128,1792]{1,0:T(8,128)(2,1)}, f32[1792,256]{1,0:T(8,128)}) custom-call(bf16[128,1792]{1,0:T(8,128)(2,1)S(1)} %get-tuple-element.6.a, bf16[128,1792]{1,0:T(8,128)(2,1)S(1)} %get-tuple-element.7.b, f32[1792,256]{1,0:T(8,128)S(1)} %get-tuple-element.8.c), custom_call_target="tpu_custom_call" | custom-call | tf_op jit(solution)/shard_map/hand_out/pallas_call | solution.py:317

commit v3 on v2

--- a/solution.py
+++ b/solution.py
@@ -13,7 +13,7 @@
 def kernel(
     d_ref, g_ref, u_ref, w_ref, gg_ref, gu_ref, gd_ref,
     gv, uv, s1, s2, xb, ht, wb, dh, rra, rrb, rla, rlb, cs, cr, k0, ys, yr,
-    lsem, xs, xr, ags, agr, rss, rsr, ws, wr, gs, gr,
+    lsem, ss, xr, agr, rsr, wr, gr,
 ):
     g, m = lax.axis_index("dp"), lax.axis_index("mp")
     yh, z, c = g // 16, (g // 2) % 8, g % 2
@@ -29,14 +29,11 @@
     cdev = ((yh * 8 + z) * 2 + 1 - c, m)
     ldev = (g, (1 - yl) * 4 + x)
 
-    sent = []
-
     def send(src, dst, ssem, rsem, to):
         cp = pltpu.make_async_remote_copy(
             src_ref=src, dst_ref=dst, send_sem=ssem, recv_sem=rsem, device_id=to, device_id_type=MESH
         )
         cp.start()
-        sent.append(cp)
         return cp
 
     barrier = pltpu.get_barrier_semaphore()
@@ -65,6 +62,27 @@
     def ht_cols(k):
         return pl.ds(pl.multiple_of(((z + k) % 8) * TOK, TOK), TOK)
 
+    pl.semaphore_wait(barrier, len(friends))
+
+    for k in (4, 3, 5, 2, 6, 1, 7):
+        for h in range(2):
+            cols = pl.ds(pl.multiple_of(h * 4096 + ((z + k) % 8) * 512, 512), 512)
+            send(
+                d_ref.at[:, cols], xb.at[z, myrows, pl.ds(h * 512, 512)],
+                ss.at[0], xr.at[7], zdev(k),
+            )
+
+    wrows = (pl.ds(0, HF), pl.ds(HF, HF))
+
+    def wsend_y(i):
+        return send(w_ref.at[wrows[i]], wb.at[wrows[i], own_b], ss.at[1], wr.at[i], ydev)
+
+    def wsend_c(i):
+        wc.append(send(wb.at[wrows[i], oth_b], wb.at[wrows[i], oth_b], ss.at[1], wr.at[3 + i], cdev))
+
+    wy = [wsend_y(0)]
+    wc = [send(w_ref, wb.at[:, own_b], ss.at[1], wr.at[2], cdev)]
+
     cpg.wait()
     cpu.wait()
 
@@ -79,34 +97,13 @@
         s2[:, sl] = up * sig * (1.0 + gate * (1.0 - sig))
         ht[sl, ht_cols(0)] = (a * up).T.astype(jnp.bfloat16)
 
-    pl.semaphore_wait(barrier, len(friends))
-
-    a2a = []
-    for k in (4, 3, 5, 2, 6, 1, 7):
-        for h in range(2):
-            cols = pl.ds(pl.multiple_of(h * 4096 + ((z + k) % 8) * 512, 512), 512)
-            i = (k - 1) * 2 + h
-            a2a.append(
-                send(
-                    d_ref.at[:, cols], xb.at[z, myrows, pl.ds(h * 512, 512)],
-                    xs.at[i], xr.at[i], zdev(k),
-                )
-            )
-
-    def wsend_y(i):
-        rows = (pl.ds(0, 768), pl.ds(768, 1024))[i]
-        return send(w_ref.at[rows], wb.at[rows, own_b], ws.at[i], wr.at[i], ydev)
-
-    wy = [wsend_y(0)]
-    wc = [send(w_ref, wb.at[:, own_b], ws.at[2], wr.at[2], cdev)]
-
     half = [pl.ds(0, HF), pl.ds(HF, HF)]
     agright, agleft = [], []
 
     def ag(lst, k, hh, to, base):
         i = base + len(lst)
         lst.append(
-            send(ht.at[half[hh], ht_cols(k)], ht.at[half[hh], ht_cols(k)], ags.at[i], agr.at[i], to)
+            send(ht.at[half[hh], ht_cols(k)], ht.at[half[hh], ht_cols(k)], ss.at[2], agr.at[i], to)
         )
 
     for hh in range(2):
@@ -122,14 +119,14 @@
 
     for cp in cpx:
         cp.wait()
-    for cp in a2a:
-        cp.wait_recv()
+    seven = xb.at[pl.ds(0, 7), pl.ds(0, 16), :]
+    pltpu.make_async_copy(seven, seven, xr.at[7]).wait()
 
     def slot(l, xx):
         return xb.at[:, pl.ds(pl.multiple_of((l * 4 + xx % 4) * 16, 16), 16), :]
 
     def xsend(l, xx, i, to):
-        return send(slot(l, xx), slot(l, xx), xs.at[14 + i], xr.at[14 + i], to)
+        return send(slot(l, xx), slot(l, xx), ss.at[3], xr.at[i], to)
 
     xy = xsend(yl, x, 0, ldev)
     xa = [xsend(yl, x, 1, xdev(1)), xsend(yl, x, 2, xdev(3))]
@@ -141,13 +138,14 @@
         cp.wait_recv()
     xf = [xsend(yl, x + 3, 5, xdev(1))]
     ag_event(1)
+    wy[0].wait_recv()
+    wsend_c(0)
     for cp in xb2:
         cp.wait_recv()
     xf.append(xsend(1 - yl, x + 1, 6, xdev(3)))
     ag_event(2)
-    for cp in wy:
-        cp.wait_recv()
-    wc.append(send(wb.at[:, oth_b], wb.at[:, oth_b], ws.at[3], wr.at[3], cdev))
+    wy[1].wait_recv()
+    wsend_c(1)
     ag_event(3)
     for cp in xf:
         cp.wait_recv()
@@ -155,8 +153,7 @@
     for cp in wc:
         cp.wait_recv()
 
-    @pl.loop(0, F // 256)
-    def _(i):
+    def partial(i):
         sl = pl.ds(pl.multiple_of(i * 256, 256), 256)
         r = lax.dot_general(
             xb[...].reshape(8 * TOK, 1024), wb[sl, :], (((1,), (1,)), ((), ())),
@@ -164,7 +161,9 @@
         )
         dh[:, :, sl] = r.astype(jnp.bfloat16).reshape(8, TOK, 256)
 
+    pl.loop(0, 2)(partial)
     ag_event(4)
+    pl.loop(2, F // 256)(partial)
     rsright, rsleft = [], []
     rbuf = {("r", 0): rra, ("r", 1): rrb, ("l", 0): rla, ("l", 1): rlb}
 
@@ -178,7 +177,7 @@
         lst.append(
             send(
                 dh.at[(z + (k if right else -k)) % 8, :, half[hh]], buf.at[i // 2],
-                rss.at[j], rsr.at[j], zdev(1) if right else zdev(7),
+                ss.at[4], rsr.at[j], zdev(1) if right else zdev(7),
             )
         )
 
@@ -223,7 +222,7 @@
 
         for h in range(2):
             cps.append(
-                send(cs.at[n, half[h], :], cr.at[n, half[h], :], gs.at[2 * n + h], gr.at[2 * n + h], cdev)
+                send(cs.at[n, half[h], :], cr.at[n, half[h], :], ss.at[5], gr.at[2 * n + h], cdev)
             )
         return cps
 
@@ -234,12 +233,12 @@
 
     c0 = to_core(0, 1 - yh)
     keep(k0, 1 - yh)
+    rs_event(0)
     yy = []
     for h in range(2):
         c0[h].wait_recv()
         ys[half[h], :] = (k0[half[h], :] + cr[0, half[h], :].astype(jnp.float32)).astype(jnp.bfloat16)
-        yy.append(send(ys.at[half[h], :], yr.at[half[h], :], gs.at[4 + h], gr.at[4 + h], ydev))
-    rs_event(0)
+        yy.append(send(ys.at[half[h], :], yr.at[half[h], :], ss.at[6], gr.at[4 + h], ydev))
     c1 = to_core(1, yh)
     keep(gd_ref, yh)
     rs_event(1)
@@ -266,15 +265,19 @@
         )
         gu_ref[:, half[hh]] = (total * s1[:, half[hh]]).astype(jnp.bfloat16)
         gg_ref[:, half[hh]] = (total * s2[:, half[hh]]).astype(jnp.bfloat16)
-    for cp in sent:
-        cp.wait_send()
+    for i, ref in enumerate(
+        (
+            d_ref.at[:, pl.ds(0, 7168)], wb.at[:, pl.ds(0, 768)], ht.at[:, pl.ds(0, 896)],
+            xb.at[:, pl.ds(0, 112), :], dh.at[pl.ds(0, 7)], cs, ys,
+        )
+    ):
+        pltpu.make_async_copy(ref, ref, ss.at[i]).wait()
 
 
 def hand_out(a, b, c, ao, bo, co, sem):
-    cps = [pltpu.make_async_copy(a, ao, sem.at[0]), pltpu.make_async_copy(b, bo, sem.at[1])]
-    for i in range(4):
-        rows = pl.ds(i * (F // 4), F // 4)
-        cps.append(pltpu.make_async_copy(c.at[rows], co.at[rows], sem.at[2 + i]))
+    cps = [
+        pltpu.make_async_copy(src, dst, sem.at[i]) for i, (src, dst) in enumerate(((a, ao), (b, bo), (c, co)))
+    ]
     for cp in cps:
         cp.start()
     for cp in cps:
@@ -303,8 +306,7 @@
             V((4, TOK, HF), bf), V((3, TOK, HF), bf), V((3, TOK, HF), bf), V((4, TOK, HF), bf),
             V((2, F, DB), bf), V((2, F, DB), bf), V((F, DB), f32),
             V((F, DB), bf), V((F, DB), bf),
-            dma((5,)), dma((21,)), dma((21,)), dma((14,)), dma((14,)), dma((14,)), dma((14,)),
-            dma((4,)), dma((4,)), dma((6,)), dma((6,)),
+            dma((5,)), dma((7,)), dma((8,)), dma((14,)), dma((14,)), dma((5,)), dma((6,)),
         ],
         compiler_params=pltpu.CompilerParams(
             collective_id=0, has_side_effects=True, vmem_limit_bytes=60 << 20
@@ -319,7 +321,7 @@
         out_shape=shapes,
         in_specs=[vm] * 3,
         out_specs=(hbm, hbm, hbm),
-        scratch_shapes=[dma((6,))],
+        scratch_shapes=[dma((3,))],
         compiler_params=pltpu.CompilerParams(vmem_limit_bytes=1 << 20),
         name="hand_out",
     )(*res)

time: 90.3 us -> 87.5 us (0.969)
  Pallas kernels: 89.5 us -> 86.3 us
    pallas_call x1, Pallas kernels: 88 us -> 84.7 us  [on_device(): pl.pallas_call(kernel, out_shape=tuple((V(t.shape, t.dtype) for t in shap...]
where the time goes in v3:
time: 87.5 us; the launch traced here: 86.9 us
  Pallas kernels  86.3 us (99%)
    pallas_call x1, Pallas kernels, on_device(): pl.pallas_call(kernel, out_shape=tuple((V(t.shape, t.dtype) for t in shap...  84.7 us

profile of v3, /device:TPU:1, one launch (start us, length us, event | category | flops | bytes accessed | tf_op | source)
XLA Modules:
  0.0 86.9 jit_solution(17661953756618297912)
XLA Ops:
  0.6 84.7 %glu_down_backward.1 = (bf16[128,1792]{1,0:T(8,128)(2,1)S(1)}, bf16[128,1792]{1,0:T(8,128)(2,1)S(1)}, f32[1792,256]{1,0:T(8,128)S(1)}) custom-call(bf16[16,8192]{1,0:T(8,128)(2,1)} %d_ref.1, bf16[128,1792]{1,0:T(8,128)(2,1)} %g_ref.1, bf16[128,1792]{1,0:T(8,128)(2,1)} %u_ref.1, bf16[1792,256]{1,0:T(8,128)(2,1)} %w_ref.1), custom_call_target="tpu_custom_call" | custom-call | flops 7516192768 | bytes 6291456 | tf_op jit(solution)/shard_map/glu_down_backward/pallas_call | solution.py:298
  85.4 1.6 %hand_out.1 = (bf16[128,1792]{1,0:T(8,128)(2,1)}, bf16[128,1792]{1,0:T(8,128)(2,1)}, f32[1792,256]{1,0:T(8,128)}) custom-call(bf16[128,1792]{1,0:T(8,128)(2,1)S(1)} %get-tuple-element.6.a, bf16[128,1792]{1,0:T(8,128)(2,1)S(1)} %get-tuple-element.7.b, f32[1792,256]{1,0:T(8,128)S(1)} %get-tuple-element.8.c), custom_call_target="tpu_custom_call" | custom-call | tf_op jit(solution)/shard_map/hand_out/pallas_call | solution.py:319

commit v4 on v3

v4 whole, which is shorter than its diff:
```python
import jax
import jax.numpy as jnp
from jax import lax
from jax.experimental import pallas as pl
from jax.experimental.pallas import tpu as pltpu
from jax.sharding import PartitionSpec as P

MESH = pl.DeviceIdType.MESH
TOK, F, DB, HF = 128, 1792, 256, 896
D = 8192


def kernel(
    d_ref, g_ref, u_ref, w_ref, gg_ref, gu_ref, gd_ref,
    dv, gv, uv, s1, s2, tot, xb, ht, wb, dh, rra, rrb, rla, rlb, cs, cr, k0, ys, yr,
    lsem, ss, xr, agr, rsr, wr, gr,
):
    g, m = lax.axis_index("dp"), lax.axis_index("mp")
    yh, z, c = g // 16, (g // 2) % 8, g % 2
    yl, x = m // 4, m % 4

    def zdev(k):
        return ((yh * 8 + (z + k) % 8) * 2 + c, m)

    def xdev(k):
        return (g, yl * 4 + (x + k) % 4)

    ydev = (((1 - yh) * 8 + z) * 2 + c, m)
    cdev = ((yh * 8 + z) * 2 + 1 - c, m)
    ldev = (g, (1 - yl) * 4 + x)

    def send(src, dst, ssem, rsem, to):
        cp = pltpu.make_async_remote_copy(
            src_ref=src, dst_ref=dst, send_sem=ssem, recv_sem=rsem, device_id=to, device_id_type=MESH
        )
        cp.start()
        return cp

    def got(ref, sem):
        pltpu.make_async_copy(ref, ref, sem).wait()

    barrier = pltpu.get_barrier_semaphore()
    friends = [zdev(k) for k in (4, 3, 5, 2, 6, 1, 7)] + [xdev(1), xdev(3), ydev, cdev, ldev]
    for f in friends:
        pl.semaphore_signal(barrier, inc=1, device_id=f, device_id_type=MESH)

    cpg = pltpu.make_async_copy(g_ref, gv, lsem.at[0])
    cpu = pltpu.make_async_copy(u_ref, uv, lsem.at[1])
    own_b = pl.ds(pl.multiple_of((yh * 2 + c) * DB, DB), DB)
    oth_b = pl.ds(pl.multiple_of(((1 - yh) * 2 + c) * DB, DB), DB)
    cpw = pltpu.make_async_copy(w_ref, wb.at[:, own_b], lsem.at[2])
    cpd = pltpu.make_async_copy(d_ref, dv, lsem.at[4])
    cpd.start()
    cpg.start()
    cpu.start()
    cpw.start()
    myrows = pl.ds(pl.multiple_of(m * 16, 16), 16)
    for h in range(2):
        cols = pl.ds(pl.multiple_of(h * 4096 + z * 512, 512), 512)
        pltpu.make_async_copy(
            d_ref.at[:, cols], xb.at[z, myrows, pl.ds(h * 512, 512)], lsem.at[3]
        ).start()

    pl.semaphore_wait(barrier, len(friends))

    cpd.wait()
    for k in (4, 3, 5, 2, 6, 1, 7):
        for h in range(2):
            cols = pl.ds(pl.multiple_of(h * 4096 + ((z + k) % 8) * 512, 512), 512)
            send(
                dv.at[:, cols], xb.at[z, myrows, pl.ds(h * 512, 512)],
                ss.at[0], xr.at[4], zdev(k),
            )

    wrows = (pl.ds(0, HF), pl.ds(HF, HF))

    def wsend_y(i):
        return send(w_ref.at[wrows[i]], wb.at[wrows[i], own_b], ss.at[1], wr.at[i], ydev)

    def wsend_c(i):
        send(wb.at[wrows[i], oth_b], wb.at[wrows[i], oth_b], ss.at[1], wr.at[2], cdev)

    wy = [wsend_y(0)]
    send(w_ref, wb.at[:, own_b], ss.at[1], wr.at[2], cdev)

    cpg.wait()
    cpu.wait()

    @pl.loop(0, F // 256)
    def _(i):
        sl = pl.ds(pl.multiple_of(i * 256, 256), 256)
        gate = gv[:, sl].astype(jnp.float32)
        up = uv[:, sl].astype(jnp.float32)
        sig = jax.nn.sigmoid(gate)
        a = gate * sig
        s1[:, sl] = a
        s2[:, sl] = up * sig * (1.0 + gate * (1.0 - sig))
        ht[z, sl, :] = (a * up).T.astype(jnp.bfloat16)

    half = [pl.ds(0, HF), pl.ds(HF, HF)]

    def ag(i, u):
        for k, hh, to in ((-(i // 2), i % 2, 1), (i // 2, 1 - i % 2, 7)):
            part = ht.at[(z + k) % 8, pl.ds(hh * HF + u * 448, 448), :]
            send(part, part, ss.at[2], agr.at[2 * i + u], zdev(to))

    for i in range(2):
        ag(i, 0)
        ag(i, 1)

    def ag_event(i):
        for u in range(2):
            got(ht.at[0, pl.ds(0, HF), :], agr.at[2 * i + u])
            if i < 5:
                ag(i + 2, u)

    got(xb.at[0, pl.ds(0, 16), :], lsem.at[3])
    got(xb.at[pl.ds(0, 7), pl.ds(0, 16), :], xr.at[4])

    def slot(l, xx):
        return xb.at[:, pl.ds(pl.multiple_of((l * 4 + xx % 4) * 16, 16), 16), :]

    def xsend(l, xx, i, to):
        return send(slot(l, xx), slot(l, xx), ss.at[3], xr.at[i], to)

    xy = xsend(yl, x, 0, ldev)
    xsend(yl, x, 1, xdev(1))
    xsend(yl, x, 1, xdev(3))
    ag_event(0)
    xy.wait_recv()
    xsend(1 - yl, x, 2, xdev(1))
    xsend(1 - yl, x, 2, xdev(3))
    wy.append(wsend_y(1))
    got(xb.at[:, pl.ds(0, 32), :], xr.at[1])
    xsend(yl, x + 3, 3, xdev(1))
    ag_event(1)
    wy[0].wait_recv()
    wsend_c(0)
    ag_event(2)
    got(xb.at[:, pl.ds(0, 32), :], xr.at[2])
    xsend(1 - yl, x + 1, 3, xdev(3))
    ag_event(3)
    wy[1].wait_recv()
    wsend_c(1)
    got(xb.at[:, pl.ds(0, 32), :], xr.at[3])
    cpw.wait()
    got(wb.at[:, pl.ds(0, 512)], wr.at[2])

    def partial(hh):
        for at, n in ((0, 256), (256, 256), (512, 256), (768, 128)):
            r = lax.dot_general(
                xb[...].reshape(8 * TOK, 1024), wb[pl.ds(pl.multiple_of(hh * HF + at, 128), n), :],
                (((1,), (1,)), ((), ())), preferred_element_type=jnp.float32,
            )
            dh[:, hh, :, pl.ds(at, n)] = r.astype(jnp.bfloat16).reshape(8, TOK, n)

    pl.loop(0, 1)(partial)
    ag_event(4)
    pl.loop(1, 2)(partial)
    rbuf = {(True, 0): rra, (True, 1): rrb, (False, 0): rla, (False, 1): rlb}

    rows = [pl.ds(0, 64), pl.ds(64, 64)]

    def rs(i, right, u):
        hh = i % 2 if right else 1 - i % 2
        k = 4 - (i + 1) // 2
        send(
            dh.at[(z + (k if right else -k)) % 8, hh, rows[u]], rbuf[right, hh].at[i // 2, rows[u]],
            ss.at[4], rsr.at[2 * i + u], zdev(1) if right else zdev(7),
        )

    for i in range(2):
        for u in range(2):
            rs(i, True, u)
            rs(i, False, u)

    def rs_event(i):
        for u in range(2):
            got(dh.at[0, 0], rsr.at[2 * i + u])
            for right in (True, False):
                hh = i % 2 if right else 1 - i % 2
                k = 3 - (i + 1) // 2
                at = (z + (k if right else -k)) % 8
                dh[at, hh, rows[u]] = (
                    dh[at, hh, rows[u]].astype(jnp.float32)
                    + rbuf[right, hh][i // 2, rows[u]].astype(jnp.float32)
                ).astype(jnp.bfloat16)
                rs(i + 2, right, u)

    ag_event(5)
    ag_event(6)

    def block(by, bc, h):
        cols = pl.ds(pl.multiple_of((by * 2 + bc) * DB, DB), DB)
        return jnp.dot(
            jnp.concatenate([ht[k, hrows(h), :] for k in range(8)], axis=1),
            xb[:, :, cols].reshape(8 * TOK, DB),
            preferred_element_type=jnp.float32,
        )

    def hrows(h):
        return pl.ds(pl.multiple_of(h * HF, HF), HF)

    def to_core(n, by):
        @pl.loop(0, 2)
        def _(h):
            cs[n, hrows(h), :] = block(by, 1 - c, h).astype(jnp.bfloat16)

        for h in range(2):
            send(cs.at[n, half[h], :], cr.at[n, half[h], :], ss.at[5], gr.at[n], cdev)

    def keep(k, by):
        @pl.loop(0, 2)
        def _(h):
            k[hrows(h), :] = block(by, c, h)

    to_core(0, 1 - yh)
    keep(k0, 1 - yh)
    rs_event(0)
    yy = []
    got(cr.at[0], gr.at[0])
    for h in range(2):
        ys[half[h], :] = (k0[half[h], :] + cr[0, half[h], :].astype(jnp.float32)).astype(jnp.bfloat16)
        yy.append(send(ys.at[half[h], :], yr.at[half[h], :], ss.at[6], gr.at[2 + h], ydev))
    to_core(1, yh)
    keep(gd_ref, yh)
    rs_event(1)
    got(cr.at[1], gr.at[1])
    for h in range(2):
        gd_ref[half[h], :] += cr[1, half[h], :].astype(jnp.float32)
    rs_event(2)
    rs_event(3)
    rs_event(4)
    yy[0].wait_recv()
    def down(h):
        gd_ref[half[h], :] += yr[half[h], :].astype(jnp.float32)

    down(0)
    yy[1].wait_recv()
    down(1)
    for u in range(2):
        got(dh.at[0, 0], rsr.at[10 + u])
        for hh, right in ((0, False), (1, True)):
            tot[rows[u], half[hh]] = (
                dh[z, hh, rows[u]].astype(jnp.float32) + rbuf[right, hh][2, rows[u]].astype(jnp.float32)
            )
    for u in range(2):
        got(dh.at[0, 0], rsr.at[12 + u])
        for hh, right in ((0, True), (1, False)):
            total = tot[rows[u], half[hh]] + rbuf[right, hh][3, rows[u]].astype(jnp.float32)
            gu_ref[rows[u], half[hh]] = (total * s1[rows[u], half[hh]]).astype(jnp.bfloat16)
            gg_ref[rows[u], half[hh]] = (total * s2[rows[u], half[hh]]).astype(jnp.bfloat16)
    for i, ref in enumerate(
        (
            dv.at[:, pl.ds(0, 7168)], wb.at[:, pl.ds(0, 768)], ht.at[pl.ds(0, 7)],
            xb.at[:, pl.ds(0, 112), :], dh.at[pl.ds(0, 7)], cs, ys,
        )
    ):
        got(ref, ss.at[i])


def hand_out(a, b, c, ao, bo, co, sem):
    cps = [
        pltpu.make_async_copy(src, dst, sem.at[i]) for i, (src, dst) in enumerate(((a, ao), (b, bo), (c, co)))
    ]
    for cp in cps:
        cp.start()
    for cp in cps:
        cp.wait()


def on_device(d_out, gate_pre, up_pre, down_weight):
    bf, f32 = jnp.bfloat16, jnp.float32
    hbm = pl.BlockSpec(memory_space=pl.ANY)
    V = pltpu.VMEM
    vm = pl.BlockSpec(memory_space=V)
    dma = pltpu.SemaphoreType.DMA
    shapes = (
        jax.ShapeDtypeStruct((TOK, F), bf),
        jax.ShapeDtypeStruct((TOK, F), bf),
        jax.ShapeDtypeStruct((F, DB), f32),
    )
    res = pl.pallas_call(
        kernel,
        out_shape=tuple(V(t.shape, t.dtype) for t in shapes),
        in_specs=[hbm] * 4,
        out_specs=(vm, vm, vm),
        scratch_shapes=[
            V((16, D), bf), V((TOK, F), bf), V((TOK, F), bf), V((TOK, F), f32), V((TOK, F), f32), V((TOK, F), f32),
            V((8, TOK, 1024), bf), V((8, F, TOK), bf), V((F, 1024), bf), V((8, 2, TOK, HF), bf),
            V((4, TOK, HF), bf), V((3, TOK, HF), bf), V((3, TOK, HF), bf), V((4, TOK, HF), bf),
            V((2, F, DB), bf), V((2, F, DB), bf), V((F, DB), f32),
            V((F, DB), bf), V((F, DB), bf),
            dma((5,)), dma((7,)), dma((5,)), dma((14,)), dma((14,)), dma((3,)), dma((4,)),
        ],
        compiler_params=pltpu.CompilerParams(
            collective_id=0, has_side_effects=True, vmem_limit_bytes=60 << 20
        ),
        cost_estimate=pl.CostEstimate(
            flops=4 * 1024 * 1024 * F, bytes_accessed=6 << 20, transcendentals=TOK * F
        ),
        name="glu_down_backward",
    )(d_out, gate_pre, up_pre, down_weight)
    return pl.pallas_call(
        hand_out,
        out_shape=shapes,
        in_specs=[vm] * 3,
        out_specs=(hbm, hbm, hbm),
        scratch_shapes=[dma((3,))],
        compiler_params=pltpu.CompilerParams(vmem_limit_bytes=1 << 20),
        name="hand_out",
    )(*res)


def solution(mesh):
    return jax.shard_map(
        on_device,
        mesh=mesh,
        in_specs=(P(("dp", "mp"), None), P("dp", "mp"), P("dp", "mp"), P("mp", "dp")),
        out_specs=(P("dp", "mp"), P("dp", "mp"), P("mp", "dp")),
        check_vma=False,
    )
```

time: 87.5 us -> 87.7 us (level)
  no operation moved by 1% of the time
where the time goes in v4:
time: 87.7 us; the launch traced here: 87.6 us
  Pallas kernels  86.9 us (99%)
    pallas_call x1, Pallas kernels, on_device(): pl.pallas_call(kernel, out_shape=tuple((V(t.shape, t.dtype) for t in shap...  85.4 us

profile of v4, /device:TPU:1, one launch (start us, length us, event | category | flops | bytes accessed | tf_op | source)
XLA Modules:
  0.0 87.6 jit_solution(14403380336119431345)
XLA Ops:
  0.6 85.4 %glu_down_backward.1 = (bf16[128,1792]{1,0:T(8,128)(2,1)S(1)}, bf16[128,1792]{1,0:T(8,128)(2,1)S(1)}, f32[1792,256]{1,0:T(8,128)S(1)}) custom-call(bf16[16,8192]{1,0:T(8,128)(2,1)} %d_ref.1, bf16[128,1792]{1,0:T(8,128)(2,1)} %g_ref.1, bf16[128,1792]{1,0:T(8,128)(2,1)} %u_ref.1, bf16[1792,256]{1,0:T(8,128)(2,1)} %w_ref.1), custom_call_target="tpu_custom_call" | custom-call | flops 7516192768 | bytes 6291456 | tf_op jit(solution)/shard_map/glu_down_backward/pallas_call | solution.py:283
  86.0 1.6 %hand_out.1 = (bf16[128,1792]{1,0:T(8,128)(2,1)}, bf16[128,1792]{1,0:T(8,128)(2,1)}, f32[1792,256]{1,0:T(8,128)}) custom-call(bf16[128,1792]{1,0:T(8,128)(2,1)S(1)} %get-tuple-element.6.a, bf16[128,1792]{1,0:T(8,128)(2,1)S(1)} %get-tuple-element.7.b, f32[1792,256]{1,0:T(8,128)S(1)} %get-tuple-element.8.c), custom_call_target="tpu_custom_call" | custom-call | tf_op jit(solution)/shard_map/hand_out/pallas_call | solution.py:304

commit v5 on v4

--- a/solution.py
+++ b/solution.py
@@ -64,7 +64,7 @@
     pl.semaphore_wait(barrier, len(friends))
 
     cpd.wait()
-    for k in (4, 3, 5, 2, 6, 1, 7):
+    for k in (1, 7, 2, 6, 3, 5, 4):
         for h in range(2):
             cols = pl.ds(pl.multiple_of(h * 4096 + ((z + k) % 8) * 512, 512), 512)
             send(
@@ -99,20 +99,18 @@
 
     half = [pl.ds(0, HF), pl.ds(HF, HF)]
 
-    def ag(i, u):
+    def ag(i):
         for k, hh, to in ((-(i // 2), i % 2, 1), (i // 2, 1 - i % 2, 7)):
-            part = ht.at[(z + k) % 8, pl.ds(hh * HF + u * 448, 448), :]
-            send(part, part, ss.at[2], agr.at[2 * i + u], zdev(to))
+            part = ht.at[(z + k) % 8, half[hh], :]
+            send(part, part, ss.at[2], agr.at[i], zdev(to))
 
     for i in range(2):
-        ag(i, 0)
-        ag(i, 1)
+        ag(i)
 
     def ag_event(i):
-        for u in range(2):
-            got(ht.at[0, pl.ds(0, HF), :], agr.at[2 * i + u])
-            if i < 5:
-                ag(i + 2, u)
+        got(ht.at[0], agr.at[i])
+        if i < 5:
+            ag(i + 2)
 
     got(xb.at[0, pl.ds(0, 16), :], lsem.at[3])
     got(xb.at[pl.ds(0, 7), pl.ds(0, 16), :], xr.at[4])
@@ -159,33 +157,28 @@
     pl.loop(1, 2)(partial)
     rbuf = {(True, 0): rra, (True, 1): rrb, (False, 0): rla, (False, 1): rlb}
 
-    rows = [pl.ds(0, 64), pl.ds(64, 64)]
-
-    def rs(i, right, u):
+    def rs(i, right):
         hh = i % 2 if right else 1 - i % 2
         k = 4 - (i + 1) // 2
         send(
-            dh.at[(z + (k if right else -k)) % 8, hh, rows[u]], rbuf[right, hh].at[i // 2, rows[u]],
-            ss.at[4], rsr.at[2 * i + u], zdev(1) if right else zdev(7),
+            dh.at[(z + (k if right else -k)) % 8, hh], rbuf[right, hh].at[i // 2],
+            ss.at[4], rsr.at[i], zdev(1) if right else zdev(7),
         )
 
     for i in range(2):
-        for u in range(2):
-            rs(i, True, u)
-            rs(i, False, u)
+        rs(i, True)
+        rs(i, False)
 
     def rs_event(i):
-        for u in range(2):
-            got(dh.at[0, 0], rsr.at[2 * i + u])
-            for right in (True, False):
-                hh = i % 2 if right else 1 - i % 2
-                k = 3 - (i + 1) // 2
-                at = (z + (k if right else -k)) % 8
-                dh[at, hh, rows[u]] = (
-                    dh[at, hh, rows[u]].astype(jnp.float32)
-                    + rbuf[right, hh][i // 2, rows[u]].astype(jnp.float32)
-                ).astype(jnp.bfloat16)
-                rs(i + 2, right, u)
+        got(dh.at[0], rsr.at[i])
+        for right in (True, False):
+            hh = i % 2 if right else 1 - i % 2
+            k = 3 - (i + 1) // 2
+            at = (z + (k if right else -k)) % 8
+            dh[at, hh] = (
+                dh[at, hh].astype(jnp.float32) + rbuf[right, hh][i // 2].astype(jnp.float32)
+            ).astype(jnp.bfloat16)
+            rs(i + 2, right)
 
     ag_event(5)
     ag_event(6)
@@ -238,18 +231,14 @@
     down(0)
     yy[1].wait_recv()
     down(1)
-    for u in range(2):
-        got(dh.at[0, 0], rsr.at[10 + u])
-        for hh, right in ((0, False), (1, True)):
-            tot[rows[u], half[hh]] = (
-                dh[z, hh, rows[u]].astype(jnp.float32) + rbuf[right, hh][2, rows[u]].astype(jnp.float32)
-            )
-    for u in range(2):
-        got(dh.at[0, 0], rsr.at[12 + u])
-        for hh, right in ((0, True), (1, False)):
-            total = tot[rows[u], half[hh]] + rbuf[right, hh][3, rows[u]].astype(jnp.float32)
-            gu_ref[rows[u], half[hh]] = (total * s1[rows[u], half[hh]]).astype(jnp.bfloat16)
-            gg_ref[rows[u], half[hh]] = (total * s2[rows[u], half[hh]]).astype(jnp.bfloat16)
+    got(dh.at[0], rsr.at[5])
+    for hh, right in ((0, False), (1, True)):
+        tot[:, half[hh]] = dh[z, hh].astype(jnp.float32) + rbuf[right, hh][2].astype(jnp.float32)
+    got(dh.at[0], rsr.at[6])
+    for hh, right in ((0, True), (1, False)):
+        total = tot[:, half[hh]] + rbuf[right, hh][3].astype(jnp.float32)
+        gu_ref[:, half[hh]] = (total * s1[:, half[hh]]).astype(jnp.bfloat16)
+        gg_ref[:, half[hh]] = (total * s2[:, half[hh]]).astype(jnp.bfloat16)
     for i, ref in enumerate(
         (
             dv.at[:, pl.ds(0, 7168)], wb.at[:, pl.ds(0, 768)], ht.at[pl.ds(0, 7)],
@@ -261,7 +250,7 @@
 
 def hand_out(a, b, c, ao, bo, co, sem):
     cps = [
-        pltpu.make_async_copy(src, dst, sem.at[i]) for i, (src, dst) in enumerate(((a, ao), (b, bo), (c, co)))
+        pltpu.make_async_copy(src, dst, sem.at[i]) for i, (src, dst) in enumerate(((c, co), (a, ao), (b, bo)))
     ]
     for cp in cps:
         cp.start()
@@ -291,7 +280,7 @@
             V((4, TOK, HF), bf), V((3, TOK, HF), bf), V((3, TOK, HF), bf), V((4, TOK, HF), bf),
             V((2, F, DB), bf), V((2, F, DB), bf), V((F, DB), f32),
             V((F, DB), bf), V((F, DB), bf),
-            dma((5,)), dma((7,)), dma((5,)), dma((14,)), dma((14,)), dma((3,)), dma((4,)),
+            dma((5,)), dma((7,)), dma((5,)), dma((7,)), dma((7,)), dma((3,)), dma((4,)),
         ],
         compiler_params=pltpu.CompilerParams(
             collective_id=0, has_side_effects=True, vmem_limit_bytes=60 << 20

time: 87.7 us -> 87.6 us (level)
  no operation moved by 1% of the time
where the time goes in v5:
time: 87.6 us; the launch traced here: 87.5 us
  Pallas kernels  86.9 us (99%)
    pallas_call x1, Pallas kernels, on_device(): pl.pallas_call(kernel, out_shape=tuple((V(t.shape, t.dtype) for t in shap...  85.3 us

profile of v5, /device:TPU:1, one launch (start us, length us, event | category | flops | bytes accessed | tf_op | source)
XLA Modules:
  0.0 87.5 jit_solution(3051038312191898535)
XLA Ops:
  0.6 85.3 %glu_down_backward.1 = (bf16[128,1792]{1,0:T(8,128)(2,1)S(1)}, bf16[128,1792]{1,0:T(8,128)(2,1)S(1)}, f32[1792,256]{1,0:T(8,128)S(1)}) custom-call(bf16[16,8192]{1,0:T(8,128)(2,1)} %d_ref.1, bf16[128,1792]{1,0:T(8,128)(2,1)} %g_ref.1, bf16[128,1792]{1,0:T(8,128)(2,1)} %u_ref.1, bf16[1792,256]{1,0:T(8,128)(2,1)} %w_ref.1), custom_call_target="tpu_custom_call" | custom-call | flops 7516192768 | bytes 6291456 | tf_op jit(solution)/shard_map/glu_down_backward/pallas_call | solution.py:272
  86.0 1.5 %hand_out.1 = (bf16[128,1792]{1,0:T(8,128)(2,1)}, bf16[128,1792]{1,0:T(8,128)(2,1)}, f32[1792,256]{1,0:T(8,128)}) custom-call(bf16[128,1792]{1,0:T(8,128)(2,1)S(1)} %get-tuple-element.6.a, bf16[128,1792]{1,0:T(8,128)(2,1)S(1)} %get-tuple-element.7.b, f32[1792,256]{1,0:T(8,128)S(1)} %get-tuple-element.8.c), custom_call_target="tpu_custom_call" | custom-call | tf_op jit(solution)/shard_map/hand_out/pallas_call | solution.py:293
